TPU v7x, 256 devices: a whole 4x4x8 slice. The times are simulated.
256 devices in a mesh: feat: 16 (over y, x_hi, core), tok: 16 (over x_lo, z).
Axes of the slice: x: 4 (x_hi: 2, x_lo: 2; x = x_hi * 2 + x_lo), y: 4, z: 8, core: 2. Of those that a mesh axis runs over, the one named last changes fastest.
Arguments:
- key_rows: bfloat16 [2, 2048, 2048], P(None, 'tok'), may hold values from -6 to 6
- value_rows: bfloat16 [2, 2048, 2048], P(None, 'tok', 'feat'), may hold values from -6 to 6
- queries: bfloat16 [2, 2048, 2048], P(None, 'tok'), may hold values from -6 to 6
- output_cot: bfloat16 [2, 2048, 2048], P(None, 'tok'), may hold values from -3 to 3
- token_rates: float32 [2, 2048], P(None, 'tok'), may hold values from 0.002 to 0.02
- w_first: bfloat16 [2, 2048, 8192], P(None, None, 'feat'), may hold values from -0.125 to 0.125
- w_second: bfloat16 [2, 2048, 8192], P(None, None, 'feat'), may hold values from -0.0625 to 0.0625
- final_first: bfloat16 [2048, 8192], P('tok', 'feat'), may hold values from -24 to 24
- final_second: bfloat16 [2048, 8192], P('tok', 'feat'), may hold values from -24 to 24
Outputs:
- grad_keys: bfloat16 [2, 2048, 2048], P(None, 'tok', 'feat')
- grad_values: bfloat16 [2, 2048, 2048], P(None, 'tok', 'feat')
- grad_queries: bfloat16 [2, 2048, 2048], P(None, 'tok', 'feat')
- grad_first: float32 [2048, 8192], P('tok', 'feat')
- grad_second: float32 [2048, 8192], P('tok', 'feat')
All inputs are finite; a program needn't handle non-finite values.
Results may differ from a plain program's by a relative error of at most 0.0095.
Values may be sent and summed in bfloat16 or wider, within the bound.
No kernel may reach another device: no remote copies, remote signals or barrier semaphores. Data moves between devices by JAX's collectives and lax.ppermute only.
A program may use at most 128 MiB of HBM per device.

v0:
```python
import jax
import jax.numpy as jnp
from jax import lax
from jax.sharding import PartitionSpec as P

momentum_decay = 0.9


def silu_terms(hidden):
    sig = jax.nn.sigmoid(hidden)
    slope = sig * (1.0 + hidden * (1.0 - sig))
    curve = sig * (1.0 - sig) * (2.0 + hidden * (1.0 - 2.0 * sig))
    return (hidden * sig, slope, curve)


def reduce_terms(term_fn, slice_rows):
    return lax.psum_scatter(
        term_fn(jnp.int32(0), slice_rows * lax.axis_size("tok")),
        "tok",
        scatter_dimension=0,
        tiled=True,
    )


def block_backward(keyb, value_share, queryb, cotb, rateb, inner, outer, panel_first, panel_second):
    share_width = value_share.shape[1]
    feat_offset = lax.axis_index("feat") * share_width
    block_tokens = rateb.shape[0] * lax.axis_size("tok")
    rate_column = (rateb / block_tokens)[:, None]
    pre = jnp.dot(keyb, inner, preferred_element_type=jnp.float32)
    act, slope, curve = silu_terms(pre)
    act_b = act.astype(jnp.bfloat16)
    predicted = jnp.dot(act_b, outer.T, preferred_element_type=jnp.float32)
    placed = lax.dynamic_update_slice_in_dim(
        jnp.zeros_like(predicted), value_share.astype(jnp.float32), feat_offset, 1
    )
    error_full = lax.psum(predicted - placed, "feat")
    weighted = (rate_column * error_full).astype(jnp.bfloat16)
    gated = jnp.dot(weighted, outer, preferred_element_type=jnp.float32)
    delta_b = (gated * slope).astype(jnp.bfloat16)
    query_pre = jnp.dot(queryb, inner, preferred_element_type=jnp.float32)
    read, query_slope, unused = silu_terms(query_pre)
    read_b = read.astype(jnp.bfloat16)
    back_delta = jnp.dot(keyb, panel_first, preferred_element_type=jnp.float32)
    back_gated = (back_delta * slope).astype(jnp.bfloat16)
    back_weighted = jnp.dot(act_b, panel_second.T, preferred_element_type=jnp.float32)
    back_weighted = back_weighted + jnp.dot(back_gated, outer.T, preferred_element_type=jnp.float32)
    back_error = rate_column * lax.psum(back_weighted, "feat")
    back_out = back_error.astype(jnp.bfloat16)
    own_error = lax.dynamic_slice_in_dim(back_error, feat_offset, share_width, 1)
    grad_value = (-own_error).astype(jnp.bfloat16)
    back_act = jnp.dot(weighted, panel_second, preferred_element_type=jnp.float32)
    back_act = back_act + jnp.dot(back_out, outer, preferred_element_type=jnp.float32)
    back_pre = (back_act * slope + back_delta * gated * curve).astype(jnp.bfloat16)
    back_read = (jnp.dot(cotb, outer, preferred_element_type=jnp.float32) * query_slope).astype(
        jnp.bfloat16
    )
    key_part = jnp.dot(delta_b, panel_first.T, preferred_element_type=jnp.float32)
    key_part = key_part + jnp.dot(back_pre, inner.T, preferred_element_type=jnp.float32)
    query_part = jnp.dot(back_read, inner.T, preferred_element_type=jnp.float32)
    key_share, query_share = (
        lax.psum_scatter(key_part, "feat", scatter_dimension=1, tiled=True),
        lax.psum_scatter(query_part, "feat", scatter_dimension=1, tiled=True),
    )
    left_first = jnp.concatenate([keyb, queryb], axis=0)
    right_first = jnp.concatenate([back_pre, back_read], axis=0)
    left_second = jnp.concatenate([back_out, weighted, cotb], axis=0)
    right_second = jnp.concatenate([act_b, back_gated, read_b], axis=0)

    def term_fn(start, count):
        term_first = jnp.dot(left_first.T, right_first, preferred_element_type=jnp.float32)
        term_second = jnp.dot(left_second.T, right_second, preferred_element_type=jnp.float32)
        return jnp.concatenate([term_first, term_second], axis=1)

    grads = (key_share.astype(jnp.bfloat16), grad_value, query_share.astype(jnp.bfloat16))
    return (grads, term_fn)


def on_device(
    key_rows,
    value_rows,
    queries,
    output_cot,
    token_rates,
    w_first,
    w_second,
    final_first,
    final_second,
):
    updates = key_rows.shape[0]
    width = w_first.shape[2]
    slice_rows = final_first.shape[0]
    start_final = jnp.concatenate([final_first, final_second], axis=1)
    carry_part = start_final.astype(jnp.float32)
    moment_part = carry_part
    key_list = [None] * updates
    value_list = [None] * updates
    query_list = [None] * updates
    for step_index in reversed(range(updates)):
        if step_index < updates - 1:
            moment_part = carry_part + momentum_decay * moment_part
        panels = lax.all_gather((-moment_part).astype(jnp.bfloat16), "tok", axis=0, tiled=True)
        grads, term_fn = block_backward(
            key_rows[step_index],
            value_rows[step_index],
            queries[step_index],
            output_cot[step_index],
            token_rates[step_index],
            w_first[step_index],
            w_second[step_index],
            panels[:, :width],
            panels[:, width:],
        )
        key_list[step_index] = grads[0]
        value_list[step_index] = grads[1]
        query_list[step_index] = grads[2]
        carry_part = carry_part + reduce_terms(term_fn, slice_rows)
    return (
        jnp.stack(key_list),
        jnp.stack(value_list),
        jnp.stack(query_list),
        carry_part[:, :width],
        carry_part[:, width:],
    )


def solution(mesh):
    return jax.shard_map(
        on_device,
        mesh=mesh,
        in_specs=(
            P(None, "tok", None),
            P(None, "tok", "feat"),
            P(None, "tok", None),
            P(None, "tok", None),
            P(None, "tok"),
            P(None, None, "feat"),
            P(None, None, "feat"),
            P("tok", "feat"),
            P("tok", "feat"),
        ),
        out_specs=(
            P(None, "tok", "feat"),
            P(None, "tok", "feat"),
            P(None, "tok", "feat"),
            P("tok", "feat"),
            P("tok", "feat"),
        ),
        check_vma=False,
    )
```

profile of v0, /device:TPU:1, one launch (start us, length us, event | category | flops | bytes accessed | tf_op | source)
XLA Modules:
  0.0 1050.6 jit_solution(18005726568671826942)
XLA Ops:
  7.2 1.1 copy.15
  8.3 1.0 copy.14
  9.4 0.8 fusion.126
  10.3 0.8 convert_dynamic-update-slice_fusion
  11.1 2.2 fusion.13
  13.3 80.4 %all-gather.3.cloned.1.call-done = bf16[2048,1024]{0,1:T(8,128)(2,1)} async-done(((bf16[128,1024]{0,1:T(8,128)(2,1)}), bf16[2048,1024]{0,1:T(8,128)(2,1)}) %all-gather.3.cloned.1.call-update) | async-done | bytes 4194320 | tf_op jit(solution)/shard_map/all_gather | solution.py:102
  93.8 3.3 multiply_convert_fusion.6
  97.0 1.8 convolution_subtract_fusion
  98.8 0.9 copy-done.9
  100.2 1.8 convolution_add_fusion.3
  102.1 2.9 multiply_convert_fusion.5
  105.6 1.0 slice_bitcast_fusion.1
  106.8 0.5 copy-done.14
  107.4 154.4 %all-reduce.7.cloned.1.call-done = (f32[128,2048]{1,0:T(8,128)}, f32[128,2048]{1,0:T(8,128)}) async-done(((f32[128,2048]{1,0:T(8,128)}, f32[128,2048]{1,0:T(8,128)}), (f32[128,2048]{1,0:T(8,128)}, f32[128,2048]{1,0:T(8,128)})) %all-reduce.7.cloned.1.call-update) | async-done | bytes 2097168 | tf_op jit(solution)/shard_map/psum | solution.py:37
  261.8 2.0 fusion.164
  263.8 0.8 copy-done.2
  265.8 1.3 fusion.46
  267.1 0.9 copy-done.10
  268.1 0.9 fusion.102
  269.0 0.8 fusion.118
  269.8 3.9 pad_maximum_fusion
  273.8 102.6 %reduce-scatter.7.cloned.1.call-done = f32[128,1024]{0,1:T(8,128)} async-done(((f32[2048,1024]{0,1:T(8,128)}), f32[128,1024]{0,1:T(8,128)}) %reduce-scatter.7.cloned.1.call-update) | async-done | bytes 524304 | tf_op jit(solution)/shard_map/reduce_scatter | solution.py:17
  376.4 1.8 fusion.129
  378.4 0.8 convert_dynamic-update-slice_fusion.1
  379.2 2.9 fusion.28
  382.1 73.7 %all-gather.5.cloned.1.call-done = bf16[2048,1024]{0,1:T(8,128)(2,1)} async-done(((bf16[128,1024]{0,1:T(8,128)(2,1)}), bf16[2048,1024]{0,1:T(8,128)(2,1)}) %all-gather.5.cloned.1.call-update) | async-done | bytes 4194320 | tf_op jit(solution)/shard_map/all_gather | solution.py:102
  455.9 3.4 multiply_convert_fusion.4
  459.3 1.8 convolution_subtract_fusion.1
  461.1 0.9 copy-done.11
  462.4 1.9 convolution_add_fusion.2
  464.4 3.5 fusion.8
  468.1 2.2 multiply_convert_fusion.2
  470.4 0.5 copy-done.4
  470.9 1.7 fusion.99
  472.9 1.8 fusion.23
  474.7 2.1 fusion.38
  476.8 3.4 convolution_add_fusion
  480.3 143.8 %all-reduce.5.cloned.1.call-done = (f32[128,2048]{1,0:T(8,128)}, f32[128,2048]{1,0:T(8,128)}) async-done(((f32[128,2048]{1,0:T(8,128)}, f32[128,2048]{1,0:T(8,128)}), (f32[128,2048]{1,0:T(8,128)}, f32[128,2048]{1,0:T(8,128)})) %all-reduce.5.cloned.1.call-update) | async-done | bytes 2097168 | tf_op jit(solution)/shard_map/psum | solution.py:37
  624.1 3.0 fusion.163
  627.6 0.5 fusion.17
  628.0 1.4 copy-done.12
  629.5 0.5 fusion.36
  630.0 0.9 fusion.105
  631.0 1.2 copy-done.7
  632.2 1.8 convolution_add_fusion.1
  634.1 2.5 fusion.52
  636.6 0.8 fusion.122
  637.3 3.9 pad_maximum_fusion.1
  641.3 60.8 %reduce-scatter.15.cloned.1.call-done = f32[128,128]{1,0:T(8,128)} async-done(((f32[128,2048]{1,0:T(8,128)}), f32[128,128]{1,0:T(8,128)}) %reduce-scatter.15.cloned.1.call-update) | async-done | bytes 65552 | tf_op jit(solution)/shard_map/reduce_scatter | solution.py:63
  702.1 0.8 convert_bitcast_fusion
  702.9 77.4 %reduce-scatter.13.cloned.1.call-done = f32[128,128]{1,0:T(8,128)} async-done(((f32[128,2048]{1,0:T(8,128)}), f32[128,128]{1,0:T(8,128)}) %reduce-scatter.13.cloned.1.call-update) | async-done | bytes 65552 | tf_op jit(solution)/shard_map/reduce_scatter | solution.py:63
  780.3 0.8 convert_bitcast_fusion.1
  781.2 0.6 pad_maximum_fusion.5
  781.8 76.2 %reduce-scatter.11.cloned.1.call-done = f32[128,128]{1,0:T(8,128)} async-done(((f32[128,2048]{1,0:T(8,128)}), f32[128,128]{1,0:T(8,128)}) %reduce-scatter.11.cloned.1.call-update) | async-done | bytes 65552 | tf_op jit(solution)/shard_map/reduce_scatter | solution.py:62
  858.0 0.8 convert_bitcast_fusion.2
  858.9 0.8 fusion.155
  859.7 0.6 pad_maximum_fusion.4
  860.3 76.0 %reduce-scatter.9.cloned.1.call-done = f32[128,128]{1,0:T(8,128)} async-done(((f32[128,2048]{1,0:T(8,128)}), f32[128,128]{1,0:T(8,128)}) %reduce-scatter.9.cloned.1.call-update) | async-done | bytes 65552 | tf_op jit(solution)/shard_map/reduce_scatter | solution.py:62
  936.3 0.8 convert_bitcast_fusion.3
  937.2 0.6 pad_maximum_fusion.3
  937.8 103.1 %reduce-scatter.17.cloned.1.call-done = f32[128,1024]{0,1:T(8,128)} async-done(((f32[2048,1024]{0,1:T(8,128)}), f32[128,1024]{0,1:T(8,128)}) %reduce-scatter.17.cloned.1.call-update) | async-done | bytes 524304 | tf_op jit(solution)/shard_map/reduce_scatter | solution.py:17
  1040.9 1.1 fusion.140
  1042.1 0.8 copy.16
  1042.9 0.8 copy.17
  (107 shorter events, 4.7 us)
Async XLA Ops:
  7.2 86.6 %copy-start.13 = (bf16[2,128,2048]{2,1,0:T(8,128)(2,1)S(1)}, bf16[2,128,2048]{2,1,0:T(8,128)(2,1)}, u32[]{:S(2)}) copy-start(bf16[2,128,2048]{2,1,0:T(8,128)(2,1)} %param.9) | copy-start | bytes 3145732
  7.2 86.6 %all-gather.3.cloned.1.call-start = ((), (), s32[]{:S(2)}) async-start(), calls=%async_computation.6 | async-start | bytes 4456448 | tf_op jit(solution)/shard_map/all_gather | solution.py:102
  10.1 251.7 %all-reduce.7.cloned.1.call-start = ((), (), s32[]{:S(2)}) async-start(), calls=%async_computation.15 | async-start | bytes 4194304 | tf_op jit(solution)/shard_map/psum | solution.py:37
  13.3 85.5 %copy-start.34 = (f32[128,512]{1,0:T(8,128)}, f32[128,512]{1,0:T(8,128)S(1)}, u32[]{:S(2)}) copy-start(f32[128,512]{1,0:T(8,128)S(1)} %fusion.13) | copy-start | bytes 786436
  93.8 3.3 copy-start
  97.0 3.1 copy-start.24
  97.0 3.1 copy-start.29
  97.0 2.7 copy-start.9
  100.2 1.9 copy-start.31
  100.2 1.9 copy-start.15
  102.0 3.0 copy-start.18
  102.0 274.4 %reduce-scatter.7.cloned.1.call-start = ((), (), s32[]{:S(2)}) async-start(), calls=%async_computation.7 | async-start | bytes 8912896 | tf_op jit(solution)/shard_map/reduce_scatter | solution.py:17
  102.1 3.1 copy-start.1
  105.2 1.5 copy-start.16
  105.6 1.7 copy-start.14
  261.8 2.8 copy-start.2
  264.6 1.0 copy-start.25
  264.6 1.1 copy-start.26
  264.6 1.1 copy-start.30
  264.7 1.2 copy-start.40
  265.1 2.0 copy-start.32
  265.8 2.2 copy-start.10
  265.8 2.2 copy-start.35
  265.8 2.3 copy-start.39
  269.0 0.8 copy-start.19
  273.7 182.1 %all-gather.5.cloned.1.call-start = ((), (), s32[]{:S(2)}) async-start(), calls=%async_computation.8 | async-start | bytes 4456448 | tf_op jit(solution)/shard_map/all_gather | solution.py:102
  378.3 245.8 %all-reduce.5.cloned.1.call-start = ((), (), s32[]{:S(2)}) async-start(), calls=%async_computation.14 | async-start | bytes 4194304 | tf_op jit(solution)/shard_map/psum | solution.py:37
  455.9 3.5 copy-start.3
  459.3 3.1 copy-start.22
  459.3 3.1 copy-start.27
  459.3 2.7 copy-start.11
  464.3 3.8 copy-start.17
  464.3 237.7 %reduce-scatter.15.cloned.1.call-start = ((), (), s32[]{:S(2)}) async-start(), calls=%async_computation.12 | async-start | bytes 1114112 | tf_op jit(solution)/shard_map/reduce_scatter | solution.py:63
  467.9 312.4 %reduce-scatter.13.cloned.1.call-start = ((), (), s32[]{:S(2)}) async-start(), calls=%async_computation.11 | async-start | bytes 1114112 | tf_op jit(solution)/shard_map/reduce_scatter | solution.py:63
  468.1 2.8 copy-start.4
  470.4 2.5 copy-start.6
  472.9 1.9 copy-start.33
  472.9 1.9 copy-start.36
  474.6 2.2 copy-start.20
  474.7 383.3 %reduce-scatter.11.cloned.1.call-start = ((), (), s32[]{:S(2)}) async-start(), calls=%async_computation.10 | async-start | bytes 1114112 | tf_op jit(solution)/shard_map/reduce_scatter | solution.py:62
  480.3 456.0 %reduce-scatter.9.cloned.1.call-start = ((), (), s32[]{:S(2)}) async-start(), calls=%async_computation.9 | async-start | bytes 1114112 | tf_op jit(solution)/shard_map/reduce_scatter | solution.py:62
  624.1 3.0 copy-start.5
  627.1 2.9 copy-start.21
  627.1 2.4 copy-start.12
  627.1 2.4 copy-start.37
  627.6 2.5 copy-start.38
  630.0 2.2 copy-start.7
  632.2 1.9 copy-start.23
  632.2 1.9 copy-start.28
  634.0 406.9 %reduce-scatter.17.cloned.1.call-start = ((), (), s32[]{:S(2)}) async-start(), calls=%async_computation.13 | async-start | bytes 8912896 | tf_op jit(solution)/shard_map/reduce_scatter | solution.py:17
  641.2 399.7 %copy-start.8 = (f32[128,1024]{0,1:T(8,128)S(1)}, f32[128,1024]{0,1:T(8,128)}, u32[]{:S(2)}) copy-start(f32[128,1024]{0,1:T(8,128)} %reduce-scatter.7.cloned.1.call-done) | copy-start | bytes 1572868
Sparse Core Ops, SparseCore 0:
  10.3 83.4 all-gather.2
  102.1 159.6 all-reduce.6
  273.8 102.5 reduce-scatter.6
  378.6 77.2 all-gather.4
  464.5 159.6 all-reduce.4
  628.0 73.9 reduce-scatter.14
  706.7 73.6 reduce-scatter.12
  784.4 73.6 reduce-scatter.10
  862.6 73.6 reduce-scatter.8
  938.7 102.1 reduce-scatter.16
where the time goes:
time: 1050 us
  waiting for transfers between devices  949 us (90%)
  matrix products  49.3 us (5%)
  other arithmetic  24.2 us (2%)
  between operations  14.7 us (1%)
  local copies, waits for them, and re-layouts  13.2 us (1%)
    psum x2, waiting for transfers between devices, block_backward(): error_full = lax.psum(predicted - placed, 'feat')  298 us
    reduce_scatter x2, waiting for transfers between devices, reduce_terms(): lax.psum_scatter(term_fn(jnp.int32(0), slice_rows * lax.axis_size('tok'))...  206 us
    all_gather x2, waiting for transfers between devices, on_device(): lax.all_gather((-moment_part).astype(jnp.bfloat16), 'tok', axis=0, tiled=...  154 us
    reduce_scatter x2, waiting for transfers between devices, block_backward(): lax.psum_scatter(key_part, 'feat', scatter_dimension=1, tiled=True)  152 us
    reduce_scatter x2, waiting for transfers between devices, block_backward(): lax.psum_scatter(query_part, 'feat', scatter_dimension=1, tiled=True)  138 us
  transfers between devices with their start and end apart: 10, of which 10 were waited for; matrix products, arithmetic and copies ran while one was open for 4% of the time, Pallas kernels for 0%

commit v1 on v0

v1 whole, which is shorter than its diff:
```python
import jax
import jax.numpy as jnp
from jax import lax
from jax.sharding import Mesh, PartitionSpec as P

momentum_decay = 0.9
F32 = jnp.float32
BF16 = jnp.bfloat16

FEAT = ("y", "xh", "core")
TOK = ("xl", "z")
PLANE = FEAT + ("xl",)


def silu_terms(hidden):
    sig = jax.nn.sigmoid(hidden)
    slope = sig * (1.0 + hidden * (1.0 - sig))
    curve = sig * (1.0 - sig) * (2.0 + hidden * (1.0 - 2.0 * sig))
    return (hidden * sig, slope, curve)


def mm(a, b):
    return jnp.dot(a, b, preferred_element_type=F32)


def mm_t(a, b):
    return lax.dot_general(a, b, (((1,), (1,)), ((), ())), preferred_element_type=F32)


def t_mm(a, b):
    return lax.dot_general(a, b, (((0,), (0,)), ((), ())), preferred_element_type=F32)


def swap(x, axis):
    return lax.ppermute(x, axis, [(0, 1), (1, 0)])


def in_order(index, mine, other, axis):
    first = jnp.where(index == 0, mine, other)
    second = jnp.where(index == 0, other, mine)
    return jnp.concatenate([first, second], axis=axis)


def with_partner(rows):
    core = lax.axis_index("core")
    xl = lax.axis_index("xl")
    quarter = rows.shape[2] // 4
    to_right = lax.dynamic_slice_in_dim(rows, core * (2 * quarter), quarter, 2)
    to_left = lax.dynamic_slice_in_dim(rows, core * (2 * quarter) + quarter, quarter, 2)
    x_chips = lax.axis_size("xh") * 2
    from_left = lax.ppermute(to_right, ("xh", "xl"), [(i, (i + 1) % x_chips) for i in range(x_chips)])
    from_right = lax.ppermute(to_left, ("xh", "xl"), [(i, (i - 1) % x_chips) for i in range(x_chips)])
    half = jnp.concatenate([from_left, from_right], axis=2)
    partner = in_order(core, half, swap(half, "core"), 2)
    return in_order(xl, rows, partner, 1)


def plane_scatter(partials, share):
    count = len(partials)
    tokens, width = partials[0].shape
    chunks = jnp.stack([partial.astype(BF16) for partial in partials])
    chunks = chunks.reshape(count, 2, tokens // 2, width // share, share).transpose(3, 1, 0, 2, 4)
    chunks = chunks.reshape(-1, count, tokens // 2, share)
    got = lax.all_to_all(chunks, PLANE, 0, 0, tiled=True)
    sums = jnp.sum(got.astype(F32), axis=0)
    return [sums[i] for i in range(count)]


def plane_gather(part):
    tokens, share = part.shape
    n = lax.axis_size(PLANE)
    got = lax.all_to_all(jnp.broadcast_to(part, (n, tokens, share)), PLANE, 0, 0, tiled=True)
    got = got.reshape(n // 2, 2, tokens, share).transpose(1, 2, 0, 3)
    return got.reshape(2 * tokens, (n // 2) * share)


def on_device(
    key_rows,
    value_rows,
    queries,
    output_cot,
    token_rates,
    w_first,
    w_second,
    final_first,
    final_second,
):
    updates, own_tokens, d_width = key_rows.shape
    share = value_rows.shape[2]
    half = w_first.shape[2] // 2
    slice_rows = final_first.shape[0]
    n_z = lax.axis_size("z")
    block_tokens = own_tokens * n_z * 2
    xl = lax.axis_index("xl")
    last = updates - 1

    def half_of(array, which):
        return lax.dynamic_slice_in_dim(array, which * half, half, array.ndim - 1)

    def both_halves(which):
        return jnp.concatenate([half_of(final_first, which), half_of(final_second, which)], axis=1)

    own_final = both_halves(xl)
    other_final = swap(both_halves(1 - xl), "xl")
    start = in_order(xl, own_final[None], other_final[None], 0)

    def gather_panels(panel):
        full = lax.all_gather(panel, "z", axis=0, tiled=False)
        full = full.transpose(1, 0, 2, 3).reshape(d_width, 2 * half)
        return full[:, :half], full[:, half:]

    inner = half_of(w_first, xl)
    outer = half_of(w_second, xl)
    rate_column = [(token_rates[u] / block_tokens)[:, None] for u in range(updates)]

    def forward(u, key):
        pre = mm(key, inner[u])
        act, slope, curve = silu_terms(pre)
        act_b = act.astype(BF16)
        error = plane_scatter([mm_t(act_b, outer[u])], share)[0] - value_rows[u].astype(F32)
        weighted_part = (rate_column[u] * error).astype(BF16)
        weighted = plane_gather(weighted_part)
        gated = mm(weighted, outer[u])
        delta_b = (gated * slope).astype(BF16)
        return act_b, slope, curve, weighted, gated, delta_b

    def read_out(u, read_rows, cot):
        query_pre = mm(read_rows, inner[u])
        read, query_slope, unused = silu_terms(query_pre)
        back_read = (mm(cot, outer[u]) * query_slope).astype(BF16)
        return read.astype(BF16), back_read

    panels = gather_panels(-start)
    keys = [None] * updates
    keys[last] = with_partner(key_rows[last:])[0]
    rest = jnp.concatenate([key_rows[:last], queries, output_cot], axis=0)
    rest = with_partner(rest)
    for u in range(last):
        keys[u] = rest[u]
    reads = [rest[last + u] for u in range(updates)]
    cots = [rest[last + updates + u] for u in range(updates)]

    carry = start.astype(F32)
    moment = carry
    key_list = [None] * updates
    value_list = [None] * updates
    query_list = [None] * updates
    hidden_sums = []
    early = forward(last, keys[last])
    for u in reversed(range(updates)):
        if u < last:
            moment = carry + momentum_decay * moment
            panels = gather_panels((-moment).astype(BF16))
        panel_first, panel_second = panels
        act_b, slope, curve, weighted, gated, delta_b = early
        read_b, back_read = read_out(u, reads[u], cots[u])
        back_delta = mm(keys[u], panel_first)
        back_gated = (back_delta * slope).astype(BF16)
        back_sum = plane_scatter(
            [mm_t(act_b, panel_second) + mm_t(back_gated, outer[u])], share
        )[0]
        back_error = rate_column[u] * back_sum
        value_list[u] = (-back_error).astype(BF16)
        back_out = plane_gather(back_error.astype(BF16))
        back_act = mm(weighted, panel_second) + mm(back_out, outer[u])
        back_pre = (back_act * slope + back_delta * gated * curve).astype(BF16)
        term_first = t_mm(keys[u], back_pre) + t_mm(reads[u], back_read)
        term_second = t_mm(back_out, act_b) + t_mm(weighted, back_gated) + t_mm(cots[u], read_b)
        terms = jnp.concatenate([term_first, term_second], axis=1).astype(BF16)
        terms = terms.reshape(2, n_z, slice_rows, 2 * half).transpose(1, 0, 2, 3)
        terms = terms.reshape(d_width, 2 * half)
        hidden_sums.append((key_list, u, (delta_b, panel_first, back_pre, inner[u])))
        hidden_sums.append((query_list, u, (back_read, inner[u])))
        if u > 0:
            terms, keys[u - 1] = lax.optimization_barrier((terms, keys[u - 1]))
            early = forward(u - 1, keys[u - 1])
        else:
            partials = []
            for unused, unused_u, factors in hidden_sums:
                pairs = list(zip(factors[::2], factors[1::2]))
                partials.append(sum(mm_t(left, right) for left, right in pairs))
            sums = plane_scatter(partials, share)
            for (where, at, unused), total in zip(hidden_sums, sums):
                where[at] = total.astype(BF16)
        total = lax.psum_scatter(terms, "z", scatter_dimension=0, tiled=True)
        carry = carry + total.astype(F32).reshape(carry.shape)

    kept = lax.dynamic_index_in_dim(carry, xl, 0, keepdims=False)
    sent = swap(lax.dynamic_index_in_dim(carry, 1 - xl, 0, keepdims=False), "xl")
    grad_first = in_order(xl, kept[:, :half], sent[:, :half], 1)
    grad_second = in_order(xl, kept[:, half:], sent[:, half:], 1)
    return (
        jnp.stack(key_list),
        jnp.stack(value_list),
        jnp.stack(query_list),
        grad_first,
        grad_second,
    )


def solution(mesh):
    n_feat, n_tok = mesh.devices.shape
    fine = Mesh(
        mesh.devices.reshape(n_feat // 4, 2, 2, 2, n_tok // 2), ("y", "xh", "core", "xl", "z")
    )
    return jax.shard_map(
        on_device,
        mesh=fine,
        in_specs=(
            P(None, TOK, None),
            P(None, TOK, FEAT),
            P(None, TOK, None),
            P(None, TOK, None),
            P(None, TOK),
            P(None, None, FEAT),
            P(None, None, FEAT),
            P(TOK, FEAT),
            P(TOK, FEAT),
        ),
        out_specs=(
            P(None, TOK, FEAT),
            P(None, TOK, FEAT),
            P(None, TOK, FEAT),
            P(TOK, FEAT),
            P(TOK, FEAT),
        ),
        check_vma=False,
    )
```

time: 1050 us -> 430 us (0.41)
  waiting for transfers between devices: 949 us -> 188 us
  starting transfers between devices: 0.6 us -> 99.3 us
  local copies, waits for them, and re-layouts: 13.2 us -> 47.7 us
    reduce_scatter x6 -> x2, waiting for transfers between devices: 496 us -> 35.6 us  [on_device(): total = lax.psum_scatter(terms, 'z', scatter_dimension=0, tiled=True)]
    psum x2 -> x0, waiting for transfers between devices: 298 us -> none  [block_backward(): error_full = lax.psum(predicted - placed, 'feat')]
    all_gather x2, waiting for transfers between devices: 154 us -> 37.5 us  [gather_panels(): full = lax.all_gather(panel, 'z', axis=0, tiled=False)]
    all_to_all x0 -> x9, waiting for transfers between devices: none -> 104 us  [the longest x5 77.7 us: plane_scatter(): got = lax.all_to_all(chunks, PLANE, 0, 0, tiled=True)]
    all_to_all x0 -> x9, starting transfers between devices: none -> 83.9 us  [the longest x5 57.6 us: plane_scatter(): got = lax.all_to_all(chunks, PLANE, 0, 0, tiled=True)]
    ppermute x0 -> x8, starting transfers between devices: none -> 15.2 us  [the longest x4 9.12 us: swap(): return lax.ppermute(x, axis, [(0, 1), (1, 0)])]
    ppermute x0 -> x8, waiting for transfers between devices: none -> 11.1 us  [the longest x4 8.78 us: swap(): return lax.ppermute(x, axis, [(0, 1), (1, 0)])]
    dot_general x30 -> x36, matrix products: 49.3 us -> 49.1 us  [the longest x14 26.6 us: mm(): return jnp.dot(a, b, preferred_element_type=F32)]
  transfers between devices with their start and end apart: 10 -> 21, of which waited for: 10 -> 14; matrix products, arithmetic and copies ran while one was open for 4% -> 18% of each run, Pallas kernels for 0% -> 0%
where the time goes in v1:
time: 430 us; the launch traced here: 425 us
  waiting for transfers between devices  188 us (44%)
  starting transfers between devices  99.3 us (23%)
  matrix products  49.1 us (11%)
  local copies, waits for them, and re-layouts  47.7 us (11%)
  other arithmetic  25.7 us (6%)
  between operations  15 us (3%)
    all_to_all x5, waiting for transfers between devices, plane_scatter(): got = lax.all_to_all(chunks, PLANE, 0, 0, tiled=True)  77.7 us
    all_to_all x5, starting transfers between devices, plane_scatter(): got = lax.all_to_all(chunks, PLANE, 0, 0, tiled=True)  57.6 us
    all_gather x2, waiting for transfers between devices, gather_panels(): full = lax.all_gather(panel, 'z', axis=0, tiled=False)  37.5 us
    reduce_scatter x2, waiting for transfers between devices, on_device(): total = lax.psum_scatter(terms, 'z', scatter_dimension=0, tiled=True)  35.6 us
    dot_general x14, matrix products, mm(): return jnp.dot(a, b, preferred_element_type=F32)  26.6 us
    all_to_all x4, waiting for transfers between devices, plane_gather(): lax.all_to_all(jnp.broadcast_to(part, (n, tokens, share)), PLANE, 0, 0, t...  26.4 us
    all_to_all x4, starting transfers between devices, plane_gather(): lax.all_to_all(jnp.broadcast_to(part, (n, tokens, share)), PLANE, 0, 0, t...  26.3 us
    unnamed x130, local copies, waits for them, and re-layouts  17.3 us
  transfers between devices with their start and end apart: 21, of which 14 were waited for; matrix products, arithmetic and copies ran while one was open for 18% of the time, Pallas kernels for 0%

profile of v1, /device:TPU:1, one launch (start us, length us, event | category | flops | bytes accessed | tf_op | source)
XLA Modules:
  0.0 425.1 jit_solution(15329556102425222807)
XLA Ops:
  8.3 2.1 collective-permute-start.3
  10.4 2.4 collective-permute-done.3
  15.0 1.5 collective-permute-start
  16.6 1.9 collective-permute-start.1
  18.5 2.3 collective-permute-done
  20.8 4.4 %collective-permute-start.2 = (bf16[1,128,1024]{2,1,0:T(8,128)(2,1)S(1)}, bf16[1,128,1024]{2,1,0:T(8,128)(2,1)S(1)}, u32[]{:S(2)}, u32[]{:S(2)}) collective-permute-start(bf16[1,128,1024]{2,1,0:T(8,128)(2,1)S(1)} %constant_dynamic-update-slice_fusion), channel_id=1, source_target_pairs={{0,16},{16,0},{1,17},{17,1},{2,18},{18,2},{3,19},{19,3},{4,20},{20... | collective-permute-start | bytes 786440 | tf_op jit(solution)/shard_map/ppermute | solution.py:35
  26.7 2.0 fusion.76
  28.8 1.8 fusion.8
  32.2 6.2 %all-to-all-start = ((bf16[32,1,128,128]{3,2,1,0:T(8,128)(2,1)}), bf16[32,1,128,128]{3,2,1,0:T(8,128)(2,1)S(1)}, u32[]{:S(2)}, u32[]{:S(2)}) async-start(bf16[32,1,128,128]{3,2,1,0:T(8,128)(2,1)} %bitcast.6), calls=%async_computation | async-start | bytes 2097152 | tf_op jit(solution)/shard_map/all_to_all | solution.py:64
  38.4 1.5 pad_maximum_fusion.1
  43.8 13.4 %all-gather.3.cloned.1.call-done = bf16[8,2,128,512]{3,2,0,1:T(8,128)(2,1)} async-done(((bf16[1,2,128,512]{3,2,0,1:T(8,128)(2,1)}), bf16[8,2,128,512]{3,2,0,1:T(8,128)(2,1)}) %all-gather.3.cloned.1.call-update) | async-done | bytes 2097168 | tf_op jit(solution)/shard_map/all_gather | solution.py:108
  57.2 2.5 multiply_convert_fusion.5
  60.4 1.7 fusion.15
  63.6 11.4 %all-to-all-start.2 = ((bf16[32,1,128,128]{3,2,1,0:T(8,128)(2,1)}), bf16[32,1,128,128]{3,2,1,0:T(8,128)(2,1)S(1)}, u32[]{:S(2)}, u32[]{:S(2)}) async-start(bf16[32,1,128,128]{3,2,1,0:T(8,128)(2,1)} %bitcast.18), calls=%async_computation.2 | async-start | bytes 2097152 | tf_op jit(solution)/shard_map/all_to_all | solution.py:64
  75.0 2.1 constant_dynamic-update-slice_fusion.3
  77.1 2.1 constant_dynamic-update-slice_fusion.2
  79.6 10.9 %all-to-all-done.2 = bf16[32,1,128,128]{3,2,1,0:T(8,128)(2,1)S(1)} async-done(((bf16[32,1,128,128]{3,2,1,0:T(8,128)(2,1)}), bf16[32,1,128,128]{3,2,1,0:T(8,128)(2,1)S(1)}, u32[]{:S(2)}, u32[]{:S(2)}) %all-to-all-start.2) | async-done | bytes 1048608 | tf_op jit(solution)/shard_map/all_to_all | solution.py:64
  92.1 6.9 %all-to-all-start.1 = ((bf16[32,128,128]{2,1,0:T(8,128)(2,1)}), bf16[32,128,128]{2,1,0:T(8,128)(2,1)}, u32[]{:S(2)}, u32[]{:S(2)}) async-start(bf16[32,128,128]{2,1,0:T(8,128)(2,1)} %broadcast_in_dim.16), calls=%async_computation.1 | async-start | bytes 2097152 | tf_op jit(solution)/shard_map/all_to_all | solution.py:72
  99.1 2.0 broadcast_select_fusion.3
  102.8 1.5 copy-done
  104.3 1.7 fusion.75
  106.0 8.6 %all-to-all-done.1 = bf16[32,128,128]{2,1,0:T(8,128)(2,1)} async-done(((bf16[32,128,128]{2,1,0:T(8,128)(2,1)}), bf16[32,128,128]{2,1,0:T(8,128)(2,1)}, u32[]{:S(2)}, u32[]{:S(2)}) %all-to-all-start.1) | async-done | bytes 1048608 | tf_op jit(solution)/shard_map/all_to_all | solution.py:72
  115.8 6.5 %all-to-all-start.3 = ((bf16[32,128,128]{2,1,0:T(8,128)(2,1)}), bf16[32,128,128]{2,1,0:T(8,128)(2,1)}, u32[]{:S(2)}, u32[]{:S(2)}) async-start(bf16[32,128,128]{2,1,0:T(8,128)(2,1)} %broadcast_in_dim.17), calls=%async_computation.3 | async-start | bytes 2097152 | tf_op jit(solution)/shard_map/all_to_all | solution.py:72
  122.4 2.0 fusion.21
  124.6 1.5 fusion.31
  126.1 2.1 copy.46
  128.1 2.8 fusion.46
  132.1 5.9 %all-to-all-done.3 = bf16[32,128,128]{2,1,0:T(8,128)(2,1)} async-done(((bf16[32,128,128]{2,1,0:T(8,128)(2,1)}), bf16[32,128,128]{2,1,0:T(8,128)(2,1)}, u32[]{:S(2)}, u32[]{:S(2)}) %all-to-all-start.3) | async-done | bytes 1048608 | tf_op jit(solution)/shard_map/all_to_all | solution.py:72
  138.0 1.9 copy.50
  141.0 1.8 fusion.20
  148.7 35.5 %reduce-scatter.3.cloned.1.call-done = bf16[256,512]{1,0:T(8,128)(2,1)} async-done(((bf16[2048,512]{1,0:T(8,128)(2,1)}), bf16[256,512]{1,0:T(8,128)(2,1)}) %reduce-scatter.3.cloned.1.call-update) | async-done | bytes 262160 | tf_op jit(solution)/shard_map/reduce_scatter | solution.py:185
  186.1 2.0 fusion.74
  188.1 1.7 fusion.10
  191.3 11.5 %all-to-all-start.4 = ((bf16[32,1,128,128]{3,2,1,0:T(8,128)(2,1)}), bf16[32,1,128,128]{3,2,1,0:T(8,128)(2,1)}, u32[]{:S(2)}, u32[]{:S(2)}) async-start(bf16[32,1,128,128]{3,2,1,0:T(8,128)(2,1)} %bitcast.226), calls=%async_computation.4 | async-start | bytes 2097152 | tf_op jit(solution)/shard_map/all_to_all | solution.py:64
  202.8 24.1 %all-gather.5.cloned.1.call-done = bf16[8,2,128,512]{3,2,0,1:T(8,128)(2,1)} async-done(((bf16[1,2,128,512]{3,2,0,1:T(8,128)(2,1)}), bf16[8,2,128,512]{3,2,0,1:T(8,128)(2,1)}) %all-gather.5.cloned.1.call-update) | async-done | bytes 2097168 | tf_op jit(solution)/shard_map/all_gather | solution.py:108
  226.9 2.8 multiply_convert_fusion.1
  230.2 1.7 fusion.13
  233.4 21.7 %all-to-all-start.6 = ((bf16[32,1,128,128]{3,2,1,0:T(8,128)(2,1)}), bf16[32,1,128,128]{3,2,1,0:T(8,128)(2,1)}, u32[]{:S(2)}, u32[]{:S(2)}) async-start(bf16[32,1,128,128]{3,2,1,0:T(8,128)(2,1)} %bitcast.227), calls=%async_computation.7 | async-start | bytes 2097152 | tf_op jit(solution)/shard_map/all_to_all | solution.py:64
  255.2 2.0 convert_reduce_fusion.1
  257.2 13.4 %all-to-all-done.6 = bf16[32,1,128,128]{3,2,1,0:T(8,128)(2,1)} async-done(((bf16[32,1,128,128]{3,2,1,0:T(8,128)(2,1)}), bf16[32,1,128,128]{3,2,1,0:T(8,128)(2,1)}, u32[]{:S(2)}, u32[]{:S(2)}) %all-to-all-start.6) | async-done | bytes 1048608 | tf_op jit(solution)/shard_map/all_to_all | solution.py:64
  272.6 1.5 multiply_convert_fusion.12
  275.4 6.5 %all-to-all-start.5 = ((bf16[32,128,128]{2,1,0:T(8,128)(2,1)}), bf16[32,128,128]{2,1,0:T(8,128)(2,1)}, u32[]{:S(2)}, u32[]{:S(2)}) async-start(bf16[32,128,128]{2,1,0:T(8,128)(2,1)} %broadcast_in_dim.18), calls=%async_computation.5 | async-start | bytes 2097152 | tf_op jit(solution)/shard_map/all_to_all | solution.py:72
  281.9 1.8 fusion.9
  286.5 1.7 fusion.23
  290.1 7.4 %all-to-all-done.5 = bf16[32,128,128]{2,1,0:T(8,128)(2,1)} async-done(((bf16[32,128,128]{2,1,0:T(8,128)(2,1)}), bf16[32,128,128]{2,1,0:T(8,128)(2,1)}, u32[]{:S(2)}, u32[]{:S(2)}) %all-to-all-start.5) | async-done | bytes 1048608 | tf_op jit(solution)/shard_map/all_to_all | solution.py:72
  297.6 2.0 broadcast_in_dim.19
  299.6 6.5 %all-to-all-start.7 = ((bf16[32,128,128]{2,1,0:T(8,128)(2,1)}), bf16[32,128,128]{2,1,0:T(8,128)(2,1)}, u32[]{:S(2)}, u32[]{:S(2)}) async-start(bf16[32,128,128]{2,1,0:T(8,128)(2,1)} %broadcast_in_dim.19), calls=%async_computation.8 | async-start | bytes 2097152 | tf_op jit(solution)/shard_map/all_to_all | solution.py:72
  306.1 1.9 fusion.65
  308.0 1.7 fusion.14
  311.2 2.1 copy.55
  313.3 2.8 fusion.38
  317.2 4.5 %all-to-all-done.7 = bf16[32,128,128]{2,1,0:T(8,128)(2,1)} async-done(((bf16[32,128,128]{2,1,0:T(8,128)(2,1)}), bf16[32,128,128]{2,1,0:T(8,128)(2,1)}, u32[]{:S(2)}, u32[]{:S(2)}) %all-to-all-start.7) | async-done | bytes 1048608 | tf_op jit(solution)/shard_map/all_to_all | solution.py:72
  321.7 1.9 copy.58
  325.2 1.8 fusion.58
  327.1 1.8 fusion.22
  333.9 1.5 copy.66
  335.4 1.6 copy-done.9
  337.0 1.7 fusion.12
  340.5 2.3 pad_maximum_fusion
  342.9 6.8 %all-to-all-start.8 = ((bf16[32,4,128,128]{3,2,1,0:T(8,128)(2,1)}), bf16[32,4,128,128]{3,2,1,0:T(8,128)(2,1)}, u32[]{:S(2)}, u32[]{:S(2)}) async-start(bf16[32,4,128,128]{3,2,1,0:T(8,128)(2,1)} %bitcast.221), calls=%async_computation.9 | async-start | bytes 8388608 | tf_op jit(solution)/shard_map/all_to_all | solution.py:64
  350.5 53.4 %all-to-all-done.8 = bf16[32,4,128,128]{3,2,1,0:T(8,128)(2,1)} async-done(((bf16[32,4,128,128]{3,2,1,0:T(8,128)(2,1)}), bf16[32,4,128,128]{3,2,1,0:T(8,128)(2,1)}, u32[]{:S(2)}, u32[]{:S(2)}) %all-to-all-start.8) | async-done | bytes 4194336 | tf_op jit(solution)/shard_map/all_to_all | solution.py:64
  403.9 3.0 reduce.4
  408.0 2.3 collective-permute-start.7
  411.6 5.3 %collective-permute-done.7 = f32[128,512]{1,0:T(8,128)S(1)} collective-permute-done((f32[128,512]{1,0:T(8,128)S(1)}, f32[128,512]{1,0:T(8,128)S(1)}, u32[]{:S(2)}, u32[]{:S(2)}) %collective-permute-start.7) | collective-permute-done | bytes 262176 | tf_op jit(solution)/shard_map/ppermute | solution.py:35
  (206 shorter events, 54.6 us)
Async XLA Ops:
  7.2 7.8 %slice-start = ((bf16[2,128,2048]{2,1,0:T(8,128)(2,1)}), bf16[1,128,2048]{2,1,0:T(8,128)(2,1)S(1)}, s32[]{:S(2)}) async-start(bf16[2,128,2048]{2,1,0:T(8,128)(2,1)} %param.9), calls=%async_computation.15 | async-start | bytes 1048576 | tf_op jit(solution)/shard_map/slice | solution.py:135
  7.2 50.0 %all-gather.3.cloned.1.call-start = ((), (), s32[]{:S(2)}) async-start(), calls=%async_computation.11 | async-start | bytes 2359296 | tf_op jit(solution)/shard_map/all_gather | solution.py:108
  8.3 4.5 %collective-permute-start.3 = (bf16[128,512]{1,0:T(8,128)(2,1)S(1)}, bf16[128,512]{1,0:T(8,128)(2,1)S(1)}, u32[]{:S(2)}, u32[]{:S(2)}) collective-permute-start(bf16[128,512]{1,0:T(8,128)(2,1)S(1)} %pad_maximum_fusion.11), channel_id=1, source_target_pairs={{0,8},{8,0},{1,9},{9,1},{2,10},{10,2},{3,11},{11,3},{4,12},{12,4},... | collective-permute-start | bytes 393224 | tf_op jit(solution)/shard_map/ppermute | solution.py:35
  13.5 12.9 %copy-start.21 = (bf16[2,128,2048]{2,1,0:T(8,128)(2,1)S(1)}, bf16[2,128,2048]{2,1,0:T(8,128)(2,1)}, u32[]{:S(2)}) copy-start(bf16[2,128,2048]{2,1,0:T(8,128)(2,1)} %param.9) | copy-start | bytes 3145732
  15.0 5.7 %collective-permute-start = (bf16[1,128,512]{2,1,0:T(8,128)(2,1)S(1)}, bf16[1,128,512]{2,1,0:T(8,128)(2,1)S(1)}, u32[]{:S(2)}, u32[]{:S(2)}) collective-permute-start(bf16[1,128,512]{2,1,0:T(8,128)(2,1)S(1)} %get-tuple-element.29), channel_id=1, source_target_pairs={{0,8},{8,32},{32,40},{40,0},{1,9},{9,33},{33,41},{41,1},{2,10},{10... | collective-permute-start | bytes 393224 | tf_op jit(solution)/shard_map/ppermute | solution.py:51
  16.6 4.2 collective-permute-start.1
  20.8 5.6 %collective-permute-start.2 = (bf16[1,128,1024]{2,1,0:T(8,128)(2,1)S(1)}, bf16[1,128,1024]{2,1,0:T(8,128)(2,1)S(1)}, u32[]{:S(2)}, u32[]{:S(2)}) collective-permute-start(bf16[1,128,1024]{2,1,0:T(8,128)(2,1)S(1)} %constant_dynamic-update-slice_fusion), channel_id=1, source_target_pairs={{0,16},{16,0},{1,17},{17,1},{2,18},{18,2},{3,19},{19,3},{4,20},{20... | collective-permute-start | bytes 786440 | tf_op jit(solution)/shard_map/ppermute | solution.py:35
  26.7 3.9 copy-start.31
  26.7 30.5 %copy-start.29 = (bf16[1,128,2048]{2,1,0:T(8,128)(2,1)}, bf16[1,128,2048]{2,1,0:T(8,128)(2,1)S(1)}, u32[]{:S(2)}) copy-start(bf16[1,128,2048]{2,1,0:T(8,128)(2,1)S(1)} %get-tuple-element.17) | copy-start | bytes 1572868
  28.8 111.7 %copy-start.10 = (f32[256,256]{1,0:T(8,128)}, f32[256,256]{1,0:T(8,128)S(1)}, u32[]{:S(2)}) copy-start(f32[256,256]{1,0:T(8,128)S(1)} %fusion.76) | copy-start | bytes 786436
  30.8 7.5 %copy-start.15 = (bf16[2,128,2048]{2,1,0:T(8,128)(2,1)S(1)}, bf16[2,128,2048]{2,1,0:T(8,128)(2,1)}, u32[]{:S(2)}) copy-start(bf16[2,128,2048]{2,1,0:T(8,128)(2,1)} %param.12) | copy-start | bytes 3145732
  32.2 31.4 %all-to-all-start = ((bf16[32,1,128,128]{3,2,1,0:T(8,128)(2,1)}), bf16[32,1,128,128]{3,2,1,0:T(8,128)(2,1)S(1)}, u32[]{:S(2)}, u32[]{:S(2)}) async-start(bf16[32,1,128,128]{3,2,1,0:T(8,128)(2,1)} %bitcast.6), calls=%async_computation | async-start | bytes 2097152 | tf_op jit(solution)/shard_map/all_to_all | solution.py:64
  39.9 17.3 %copy-start.32 = (bf16[1,128,2048]{2,1,0:T(8,128)(2,1)S(1)}, bf16[1,128,2048]{2,1,0:T(8,128)(2,1)}, u32[]{:S(2)}) copy-start(bf16[1,128,2048]{2,1,0:T(8,128)(2,1)} %copy-done.31) | copy-start | bytes 1572868
  41.1 33.9 %collective-permute-start.4 = (bf16[5,128,512]{2,1,0:T(8,128)(2,1)}, bf16[5,128,512]{2,1,0:T(8,128)(2,1)}, u32[]{:S(2)}, u32[]{:S(2)}) collective-permute-start(bf16[5,128,512]{2,1,0:T(8,128)(2,1)} %get-tuple-element.16), channel_id=1, source_target_pairs={{0,8},{8,32},{32,40},{40,0},{1,9},{9,33},{33,41},{41,1},{2,10},{10... | collective-permute-start | bytes 1966088 | tf_op jit(solution)/shard_map/ppermute | solution.py:51
  42.5 34.6 %collective-permute-start.5 = (bf16[5,128,512]{2,1,0:T(8,128)(2,1)}, bf16[5,128,512]{2,1,0:T(8,128)(2,1)}, u32[]{:S(2)}, u32[]{:S(2)}) collective-permute-start(bf16[5,128,512]{2,1,0:T(8,128)(2,1)} %get-tuple-element.15), channel_id=1, source_target_pairs={{0,40},{8,0},{32,8},{40,32},{1,41},{9,1},{33,9},{41,33},{2,42},{10... | collective-permute-start | bytes 1966088 | tf_op jit(solution)/shard_map/ppermute | solution.py:52
  57.2 2.5 copy-start.24
  63.6 15.8 %copy-start.55 = (f32[2,128]{1,0:T(2,128)S(1)}, f32[2,128]{1,0:T(2,128)}, u32[]{:S(2)}) copy-start(f32[2,128]{1,0:T(2,128)} %param.13) | copy-start | bytes 3076
  63.6 26.9 %all-to-all-start.2 = ((bf16[32,1,128,128]{3,2,1,0:T(8,128)(2,1)}), bf16[32,1,128,128]{3,2,1,0:T(8,128)(2,1)S(1)}, u32[]{:S(2)}, u32[]{:S(2)}) async-start(bf16[32,1,128,128]{3,2,1,0:T(8,128)(2,1)} %bitcast.18), calls=%async_computation.2 | async-start | bytes 2097152 | tf_op jit(solution)/shard_map/all_to_all | solution.py:64
  77.1 13.6 %copy-start.54 = (bf16[2,128,128]{2,1,0:T(8,128)(2,1)S(1)}, bf16[2,128,128]{2,1,0:T(8,128)(2,1)}, u32[]{:S(2)}) copy-start(bf16[2,128,128]{2,1,0:T(8,128)(2,1)} %param.10) | copy-start | bytes 196612
  79.2 19.9 %collective-permute-start.6 = (bf16[5,128,1024]{2,1,0:T(8,128)(2,1)}, bf16[5,128,1024]{2,1,0:T(8,128)(2,1)}, u32[]{:S(2)}, u32[]{:S(2)}) collective-permute-start(bf16[5,128,1024]{2,1,0:T(8,128)(2,1)} %constant_dynamic-update-slice_fusion.2), channel_id=1, source_target_pairs={{0,16},{16,0},{1,17},{17,1},{2,18},{18,2},{3,19},{19,3},{4,20},{20... | collective-permute-start | bytes 3932168 | tf_op jit(solution)/shard_map/ppermute | solution.py:35
  90.7 10.4 %copy-start.38 = (f32[128,128]{1,0:T(8,128)}, f32[128,128]{1,0:T(8,128)S(1)}, u32[]{:S(2)}) copy-start(f32[128,128]{1,0:T(8,128)S(1)} %convert_reduce_fusion.2) | copy-start | bytes 196612
  92.1 22.4 %all-to-all-start.1 = ((bf16[32,128,128]{2,1,0:T(8,128)(2,1)}), bf16[32,128,128]{2,1,0:T(8,128)(2,1)}, u32[]{:S(2)}, u32[]{:S(2)}) async-start(bf16[32,128,128]{2,1,0:T(8,128)(2,1)} %broadcast_in_dim.16), calls=%async_computation.1 | async-start | bytes 2097152 | tf_op jit(solution)/shard_map/all_to_all | solution.py:72
  99.0 2.1 copy-start.16
  99.1 2.3 copy-start.17
  115.8 22.2 %all-to-all-start.3 = ((bf16[32,128,128]{2,1,0:T(8,128)(2,1)}), bf16[32,128,128]{2,1,0:T(8,128)(2,1)}, u32[]{:S(2)}, u32[]{:S(2)}) async-start(bf16[32,128,128]{2,1,0:T(8,128)(2,1)} %broadcast_in_dim.17), calls=%async_computation.3 | async-start | bytes 2097152 | tf_op jit(solution)/shard_map/all_to_all | solution.py:72
  122.3 61.9 %reduce-scatter.3.cloned.1.call-start = ((), (), s32[]{:S(2)}) async-start(), calls=%async_computation.12 | async-start | bytes 2359296 | tf_op jit(solution)/shard_map/reduce_scatter | solution.py:185
  122.3 2.2 copy-start.1
  126.1 4.8 %copy-start.25 = (bf16[8,2,128,512]{3,2,0,1:T(8,128)(2,1)S(1)}, bf16[8,2,128,512]{3,2,0,1:T(8,128)(2,1)}, u32[]{:S(2)}) copy-start(bf16[8,2,128,512]{3,2,0,1:T(8,128)(2,1)} %all-gather.3.cloned.1.call-done) | copy-start | bytes 6291460
  128.1 2.8 copy-start.13
  141.0 1.8 copy-start.30
  141.0 1.8 copy-start.33
  142.9 1.8 copy-start.42
  144.1 1.7 copy-start.2
  148.6 36.6 %copy-start.35 = (bf16[1,1,128,512]{3,2,0,1:T(8,128)(2,1)S(1)}, bf16[1,1,128,512]{3,2,0,1:T(8,128)(2,1)}, u32[]{:S(2)}) copy-start(bf16[1,1,128,512]{3,2,0,1:T(8,128)(2,1)} %copy-done.34) | copy-start | bytes 393220
  148.6 36.6 %copy-start.37 = (bf16[1,1,128,512]{3,2,0,1:T(8,128)(2,1)S(1)}, bf16[1,1,128,512]{3,2,0,1:T(8,128)(2,1)}, u32[]{:S(2)}) copy-start(bf16[1,1,128,512]{3,2,0,1:T(8,128)(2,1)} %copy-done.36) | copy-start | bytes 393220
  148.6 78.3 %all-gather.5.cloned.1.call-start = ((), (), s32[]{:S(2)}) async-start(), calls=%async_computation.13 | async-start | bytes 2359296 | tf_op jit(solution)/shard_map/all_gather | solution.py:108
  191.3 42.1 %all-to-all-start.4 = ((bf16[32,1,128,128]{3,2,1,0:T(8,128)(2,1)}), bf16[32,1,128,128]{3,2,1,0:T(8,128)(2,1)}, u32[]{:S(2)}, u32[]{:S(2)}) async-start(bf16[32,1,128,128]{3,2,1,0:T(8,128)(2,1)} %bitcast.226), calls=%async_computation.4 | async-start | bytes 2097152 | tf_op jit(solution)/shard_map/all_to_all | solution.py:64
  226.9 2.8 copy-start.26
  229.7 2.2 copy-start.50
  233.4 37.2 %all-to-all-start.6 = ((bf16[32,1,128,128]{3,2,1,0:T(8,128)(2,1)}), bf16[32,1,128,128]{3,2,1,0:T(8,128)(2,1)}, u32[]{:S(2)}, u32[]{:S(2)}) async-start(bf16[32,1,128,128]{3,2,1,0:T(8,128)(2,1)} %bitcast.227), calls=%async_computation.7 | async-start | bytes 2097152 | tf_op jit(solution)/shard_map/all_to_all | solution.py:64
  275.4 22.2 %all-to-all-start.5 = ((bf16[32,128,128]{2,1,0:T(8,128)(2,1)}), bf16[32,128,128]{2,1,0:T(8,128)(2,1)}, u32[]{:S(2)}, u32[]{:S(2)}) async-start(bf16[32,128,128]{2,1,0:T(8,128)(2,1)} %broadcast_in_dim.18), calls=%async_computation.5 | async-start | bytes 2097152 | tf_op jit(solution)/shard_map/all_to_all | solution.py:72
  281.8 3.4 copy-start.5
  283.7 1.5 copy-start.7
  284.0 2.5 copy-start.3
  299.6 22.2 %all-to-all-start.7 = ((bf16[32,128,128]{2,1,0:T(8,128)(2,1)}), bf16[32,128,128]{2,1,0:T(8,128)(2,1)}, u32[]{:S(2)}, u32[]{:S(2)}) async-start(bf16[32,128,128]{2,1,0:T(8,128)(2,1)} %broadcast_in_dim.19), calls=%async_computation.8 | async-start | bytes 2097152 | tf_op jit(solution)/shard_map/all_to_all | solution.py:72
  306.0 100.8 %reduce-scatter.5.cloned.1.call-start = ((), (), s32[]{:S(2)}) async-start(), calls=%async_computation.14 | async-start | bytes 2359296 | tf_op jit(solution)/shard_map/reduce_scatter | solution.py:185
  306.1 1.9 copy-start.43
  311.2 4.8 %copy-start.27 = (bf16[8,2,128,512]{3,2,0,1:T(8,128)(2,1)S(1)}, bf16[8,2,128,512]{3,2,0,1:T(8,128)(2,1)}, u32[]{:S(2)}) copy-start(bf16[8,2,128,512]{3,2,0,1:T(8,128)(2,1)} %all-gather.5.cloned.1.call-done) | copy-start | bytes 6291460
  313.3 2.8 copy-start.11
  323.6 1.6 copy-start.28
  323.7 1.6 copy-start.53
  325.2 1.8 copy-start.56
  325.2 1.8 copy-start.58
  327.1 1.8 copy-start.6
  331.4 1.7 copy-start.4
  331.4 1.7 copy-start.23
  335.4 1.6 copy-start.9
  338.7 1.8 copy-start.20
  342.9 6.8 %copy-start.39 = (f32[128,128]{1,0:T(8,128)S(1)}, f32[128,128]{1,0:T(8,128)}, u32[]{:S(2)}) copy-start(f32[128,128]{1,0:T(8,128)} %copy-done.38) | copy-start | bytes 196612
  342.9 6.9 %copy-start.41 = (f32[128,128]{1,0:T(8,128)S(1)}, f32[128,128]{1,0:T(8,128)}, u32[]{:S(2)}) copy-start(f32[128,128]{1,0:T(8,128)} %copy-done.40) | copy-start | bytes 196612
  342.9 61.0 %all-to-all-start.8 = ((bf16[32,4,128,128]{3,2,1,0:T(8,128)(2,1)}), bf16[32,4,128,128]{3,2,1,0:T(8,128)(2,1)}, u32[]{:S(2)}, u32[]{:S(2)}) async-start(bf16[32,4,128,128]{3,2,1,0:T(8,128)(2,1)} %bitcast.221), calls=%async_computation.9 | async-start | bytes 8388608 | tf_op jit(solution)/shard_map/all_to_all | solution.py:64
  350.5 56.4 %copy-start.46 = (bf16[1,128,512]{2,1,0:T(8,128)(2,1)S(1)}, bf16[1,128,512]{2,1,0:T(8,128)(2,1)}, u32[]{:S(2)}) copy-start(bf16[1,128,512]{2,1,0:T(8,128)(2,1)} %get-tuple-element.30) | copy-start | bytes 393220
  350.5 56.4 %copy-start.47 = (bf16[1,128,512]{2,1,0:T(8,128)(2,1)S(1)}, bf16[1,128,512]{2,1,0:T(8,128)(2,1)}, u32[]{:S(2)}) copy-start(bf16[1,128,512]{2,1,0:T(8,128)(2,1)} %get-tuple-element.31) | copy-start | bytes 393220
  408.0 8.9 %collective-permute-start.7 = (f32[128,512]{1,0:T(8,128)S(1)}, f32[128,512]{1,0:T(8,128)S(1)}, u32[]{:S(2)}, u32[]{:S(2)}) collective-permute-start(f32[128,512]{1,0:T(8,128)S(1)} %get-tuple-element.25), channel_id=1, source_target_pairs={{0,8},{8,0},{1,9},{9,1},{2,10},{10,2},{3,11},{11,3},{4,12},{12,4},... | collective-permute-start | bytes 786440 | tf_op jit(solution)/shard_map/ppermute | solution.py:35
  (18 other events, 19.2 us)
Sparse Core Ops, SparseCore 0:
  15.1 42.0 all-gather.2
  148.7 35.4 reduce-scatter.2
  186.6 40.2 all-gather.4
  335.5 35.5 reduce-scatter.4
